TPU v7x, 128 devices: a whole 4x4x4 slice. The times are simulated.
128 devices in a mesh: dom: 32 (over z, x, core), sub: 4 (over y).
Axes of the slice: x: 4, y: 4, z: 4, core: 2. Of those that a mesh axis runs over, the one named last changes fastest.
Arguments:
- primal: bfloat16 [5, 64, 262144], P(None, None, ('dom', 'sub'))
- adjoint: bfloat16 [5, 64, 262144], P(None, None, ('dom', 'sub')), may hold values from -5 to 5
- order: int32 [262144], P(('dom', 'sub')), may hold values from 1 to 3
- faces_nbr: int32 [6, 262144], P(None, ('dom', 'sub')), may hold values from -1 to 2559, as said below
- move_elem: int32 [32768], P(('dom', 'sub')), may hold values from 0 to 2047, as said below
- move_dest: int32 [32768, 1], P(('dom', 'sub')), may hold values from 0 to 127; in each aligned block of 256 rows (0 to 255, 256 to 511, ...) at most 4 rows name the same one
- eval_op: bfloat16 [216, 64], replicated, may hold values from -0.75 to 0.75
- gradient_operator: bfloat16 [3, 125, 216], replicated, may hold values from -0.25 to 0.25
- flux_jac: float32 [3, 5, 5], replicated, may hold values from -2.5 to 2.5
- trace_op: bfloat16 [6, 16, 64], replicated, may hold values from -0.75 to 0.75
- lifting_operator: bfloat16 [6, 125, 16], replicated, may hold values from -0.625 to 0.625
- patch_from_self: bfloat16 [125, 64], replicated, may hold values from -0.75 to 0.75
- patch_from_faces: bfloat16 [6, 125, 16], replicated, may hold values from -0.625 to 0.625
Outputs:
- indicator: float32 [262144], P(('dom', 'sub'))
- shipped_adjoint: bfloat16 [5, 125, 65536], P(None, None, ('dom', 'sub'))
- shipped_primal: bfloat16 [5, 64, 65536], P(None, None, ('dom', 'sub'))
Inputs may be any that keep to these rules, and one draw needn't show every extreme that they name: faces_nbr[f, e] is -1 for a boundary face; else w, and element floor(e / 2048) * 2048 + w - 256 exists. w < 256 only for f = 4 and e among the first 256 elements of its block; w >= 2304 only for f = 5 and e among the last 256 elements of its block. `move_elem`: the 256 entries of one device are distinct. `move_dest`: among the 256 moves of one device no destination is named more than 4 times.
All inputs are finite; a program needn't handle non-finite values.
Results may differ from a plain program's by a relative error of at most 0.0053.
Values may be sent and summed in bfloat16 or wider, within the bound.
A program may use at most 192 MiB of HBM per device.

v0:
```python
import jax
import jax.numpy as jnp
from jax import lax
from jax.sharding import PartitionSpec as P


def with_halo(block, sides, width):
    for axis, dim in sides:
        count = lax.axis_size(axis)
        forward = [(i, i + 1) for i in range(count - 1)]
        backward = [(target, source) for source, target in forward]
        low = lax.ppermute(
            lax.slice_in_dim(block, block.shape[dim] - width, None, axis=dim), axis, forward
        )
        high = lax.ppermute(lax.slice_in_dim(block, 0, width, axis=dim), axis, backward)
        block = jnp.concatenate([low, block, high], axis=dim)
    return block


def mode_degree(per_side):
    modes = jnp.arange(per_side**3, dtype=jnp.int32)
    deg_one = modes // (per_side * per_side)
    deg_two = modes // per_side % per_side
    deg_three = modes % per_side
    return jnp.maximum(jnp.maximum(deg_one, deg_two), deg_three)


def lookup(windows, neighbours, variables, points):
    width = windows[0].shape[-1]
    slot_ids = jnp.arange(width, dtype=jnp.int32)[:, None]
    gathered = []
    for face in range(6):
        select = (slot_ids == neighbours[face][None, :]).astype(jnp.bfloat16)
        picked = jnp.dot(windows[face ^ 1], select, preferred_element_type=jnp.float32).astype(
            jnp.bfloat16
        )
        gathered.append(picked.reshape(2, variables, points, -1))
    return jnp.stack(gathered, axis=2)


def body(
    primal,
    adjoint,
    order,
    faces_nbr,
    move_elem,
    move_dest,
    eval_op,
    gradient_operator,
    flux_jac,
    trace_op,
    lifting_operator,
    patch_from_self,
    patch_from_faces,
):
    count = primal.shape[-1]
    variables = primal.shape[0]
    points = trace_op.shape[1]
    rim = count // 8
    keep_low = (mode_degree(4)[:, None] <= order[None, :]).astype(jnp.bfloat16)
    keep_high = (mode_degree(5)[:, None] <= order[None, :] + 1).astype(jnp.float32)
    primal_kept = primal * keep_low[None]
    adjoint_retained = adjoint * keep_low[None]
    both = jnp.stack([primal_kept, adjoint_retained])
    face_major = jnp.einsum(
        "fnb,kvbe->fkvne", trace_op, both, preferred_element_type=jnp.float32
    ).astype(jnp.bfloat16)
    face_traces = face_major.reshape(6, 2 * variables * points, count)
    padded = with_halo(face_traces, ((("dom", "sub"), 2),), rim)
    windows = [padded[face] for face in range(6)]
    exterior_trace = lookup(windows, faces_nbr, variables, points)
    interior_trace = jnp.stack([face_major[face, 0] for face in range(6)], axis=1)
    enriched_adjoint = jnp.einsum(
        "pq,cqk->cpk", patch_from_self, adjoint_retained, preferred_element_type=jnp.float32
    )
    enriched_adjoint = enriched_adjoint + jnp.einsum(
        "yzu,hyui->hzi", patch_from_faces, exterior_trace[1], preferred_element_type=jnp.float32
    )
    enriched_adjoint = (keep_high[None] * enriched_adjoint).astype(jnp.bfloat16)
    values = jnp.einsum("qb,vbe->vqe", eval_op, primal_kept, preferred_element_type=jnp.float32)
    fluxes = []
    for direction in range(3):
        mixed = jnp.einsum(
            "uv,vqe->uqe", flux_jac[direction], values, precision=lax.Precision.HIGHEST
        )
        fluxes.append(mixed + 0.25 * values[direction + 1][None] * values)
    flux_every_face = jnp.stack(fluxes).astype(jnp.bfloat16)
    residual_values = jnp.einsum(
        "lgy,luyc->ugc", gradient_operator, flux_every_face, preferred_element_type=jnp.float32
    )
    residual_values = residual_values + jnp.einsum(
        "yzu,hyui->hzi", lifting_operator, interior_trace, preferred_element_type=jnp.float32
    )
    residual_values = residual_values - jnp.einsum(
        "yzu,hyui->hzi", lifting_operator, exterior_trace[0], preferred_element_type=jnp.float32
    )
    element_error = jnp.abs(
        jnp.sum(enriched_adjoint.astype(jnp.float32) * residual_values, axis=(0, 1))
    )
    total = lax.psum(jnp.sum(element_error), ("dom", "sub"))
    devices = lax.axis_size(("dom", "sub"))
    indicator = element_error * (count * devices) / total
    moves = move_elem.shape[0]
    slots = max(2, 2 * moves // devices)
    target = move_dest[:, 0]
    onehot = (target[:, None] == jnp.arange(devices, dtype=jnp.int32)[None, :]).astype(jnp.bfloat16)
    positions = jnp.arange(moves, dtype=jnp.int32)
    earlier_mask = (positions[:, None] > positions[None, :]).astype(jnp.bfloat16)
    earlier = jnp.dot(earlier_mask, onehot, preferred_element_type=jnp.float32)
    rank = jnp.sum(earlier * onehot.astype(jnp.float32), axis=1).astype(jnp.int32)
    column = target * slots + rank
    elem_hot = (move_elem[:, None] == jnp.arange(count, dtype=jnp.int32)[None, :]).astype(
        jnp.bfloat16
    )
    column_hot = (column[:, None] == jnp.arange(devices * slots, dtype=jnp.int32)[None, :]).astype(
        jnp.bfloat16
    )
    selection = lax.dot_general(
        elem_hot, column_hot, (((0,), (0,)), ((), ())), preferred_element_type=jnp.float32
    ).astype(jnp.bfloat16)
    adjoint_rows = enriched_adjoint.reshape(-1, count)
    primal_rows = primal.reshape(-1, count)
    send_adjoint = jnp.dot(adjoint_rows, selection, preferred_element_type=jnp.float32).astype(
        jnp.bfloat16
    )
    send_primal = jnp.dot(primal_rows, selection, preferred_element_type=jnp.float32).astype(
        jnp.bfloat16
    )
    got_adjoint, got_primal = (
        lax.all_to_all(send_adjoint, ("dom", "sub"), split_axis=1, concat_axis=1, tiled=True),
        lax.all_to_all(send_primal, ("dom", "sub"), split_axis=1, concat_axis=1, tiled=True),
    )
    shipped_adjoint = got_adjoint.reshape(
        enriched_adjoint.shape[0], enriched_adjoint.shape[1], devices * slots
    )
    shipped_primal = got_primal.reshape(primal.shape[0], primal.shape[1], devices * slots)
    return (indicator, shipped_adjoint, shipped_primal)


def solution(mesh):
    return jax.shard_map(
        body,
        mesh=mesh,
        in_specs=(
            P(None, None, ("dom", "sub")),
            P(None, None, ("dom", "sub")),
            P(("dom", "sub")),
            P(None, ("dom", "sub")),
            P(("dom", "sub")),
            P(("dom", "sub"), None),
            P(),
            P(),
            P(),
            P(),
            P(),
            P(),
            P(),
        ),
        out_specs=(P(("dom", "sub")), P(None, None, ("dom", "sub")), P(None, None, ("dom", "sub"))),
        check_vma=False,
    )
```

profile of v0, /device:TPU:1, one launch (start us, length us, event | category | flops | bytes accessed | tf_op | source)
XLA Modules:
  0.0 319.0 jit_solution(17127768481389716102)
XLA Ops:
  1.5 2.0 multiply_bitcast_fusion
  3.6 1.3 convert_bitcast_fusion
  5.4 1.3 copy-done.2
  6.8 1.9 copy-done.3
  9.7 4.1 %collective-permute-start = (bf16[6,160,256]{2,1,0:T(8,128)(2,1)}, bf16[6,160,256]{2,1,0:T(8,128)(2,1)S(1)}, u32[]{:S(2)}, u32[]{:S(2)}) collective-permute-start(bf16[6,160,256]{2,1,0:T(8,128)(2,1)} %get-tuple-element.12), channel_id=1, source_target_pairs={{0,1},{1,2},{2,3},{3,4},{4,5},{5,6},{6,7},{7,8},{8,9},{9,10},{10,1... | collective-permute-start | bytes 1474568 | tf_op jit(solution)/shard_map/ppermute | solution.py:12
  13.9 3.8 %collective-permute-start.1 = (bf16[6,160,256]{2,1,0:T(8,128)(2,1)}, bf16[6,160,256]{2,1,0:T(8,128)(2,1)}, u32[]{:S(2)}, u32[]{:S(2)}) collective-permute-start(bf16[6,160,256]{2,1,0:T(8,128)(2,1)} %get-tuple-element.13), channel_id=1, source_target_pairs={{1,0},{2,1},{3,2},{4,3},{5,4},{6,5},{7,6},{8,7},{9,8},{10,9},{11,1... | collective-permute-start | bytes 1474568 | tf_op jit(solution)/shard_map/ppermute | solution.py:15
  18.9 1.3 copy-done.16
  22.1 9.8 %all-to-all-start.1 = ((bf16[320,128,4]{0,2,1:T(4,128)(2,1)}), bf16[320,128,4]{0,2,1:T(4,128)(2,1)S(1)}, u32[]{:S(2)}, u32[]{:S(2)}) async-start(bf16[320,128,4]{0,2,1:T(4,128)(2,1)} %all_to_all.14), calls=%async_computation.1 | async-start | bytes 786432 | tf_op jit(solution)/shard_map/all_to_all | solution.py:131
  38.0 1.4 convolution_bitcast_fusion
  39.4 2.9 fusion.46
  42.4 32.6 %fusion.10 = f32[216,2048,5]{1,2,0:T(8,128)} fusion(f32[5,216,2048]{2,1,0:T(8,128)S(1)} %convolution_bitcast_fusion, f32[1,5,5]{2,0,1:T(1,128)S(1)} %get-tuple-element.22), kind=kOutput, calls=%fused_computation.16 | convolution fusion | flops 132710400 | bytes 17694820 | tf_op jit(solution)/shard_map/uv,vqe->uqe/dot_general | solution.py:83
  75.0 33.1 %fusion.6 = f32[216,2048,5]{1,2,0:T(8,128)} fusion(f32[5,216,2048]{2,1,0:T(8,128)S(1)} %convolution_bitcast_fusion, f32[1,5,5]{2,0,1:T(1,128)S(1)} %get-tuple-element.24), kind=kOutput, calls=%fused_computation.12 | convolution fusion | flops 132710400 | bytes 17694820 | tf_op jit(solution)/shard_map/uv,vqe->uqe/dot_general | solution.py:83
  108.1 32.8 %fusion.8 = f32[216,2048,5]{1,2,0:T(8,128)} fusion(f32[5,216,2048]{2,1,0:T(8,128)S(1)} %convolution_bitcast_fusion, f32[1,5,5]{2,0,1:T(1,128)S(1)} %get-tuple-element.23), kind=kOutput, calls=%fused_computation.14 | convolution fusion | flops 132710400 | bytes 17694820 | tf_op jit(solution)/shard_map/uv,vqe->uqe/dot_general | solution.py:83
  142.0 30.9 %fusion.29 = (bf16[1,5,216,2048]{3,2,1,0:T(8,128)(2,1)}, bf16[1,5,216,2048]{3,2,1,0:T(8,128)(2,1)}, bf16[1,5,216,2048]{3,2,1,0:T(8,128)(2,1)}) fusion(f32[5,216,2048]{2,1,0:T(8,128)} %copy-done.1, f32[216,2048,5]{1,2,0:T(8,128)} %fusion.10, f32[216,2048]{1,0:T(8,128)S(1)} %get-tuple-element.9, f32[216,2048]{1,0:T(8,128)} %get-tuple-element.11, ...), kind=kLoop, calls=%fused_computation.44 | loop fusion | flops 19906560 | bytes 53968896 | tf_op jit(solution)/shard_map/stack | solution.py:87
  174.0 3.2 %fusion.65 = f32[5,2048,125,1]{1,2,0,3:T(8,128)} fusion(bf16[5,6,16,2048]{3,2,0,1:T(8,128)(2,1)S(1)} %fusion.54, bf16[6,125,16]{1,2,0:T(8,128)(2,1)S(1)} %copy-done.7), kind=kOutput, calls=%fused_computation.116 | convolution fusion | flops 245760000 | bytes 7110080 | tf_op jit(solution)/shard_map/yzu,hyui->hzi/dot_general | solution.py:91
  177.2 1.4 reshape.173
  178.6 3.5 %pad_maximum_fusion = bf16[6,160,2560]{2,1,0:T(8,128)(2,1)S(1)} fusion(bf16[6,160,256]{2,1,0:T(8,128)(2,1)} %collective-permute-done.1, bf16[6,160,2048]{2,1,0:T(8,128)(2,1)} %bitcast.198, bf16[6,160,256]{2,1,0:T(8,128)(2,1)S(1)} %collective-permute-done), kind=kLoop, calls=%fused_computation.43 | loop fusion | flops 14745600 | bytes 9830400 | tf_op jit(solution)/shard_map/concatenate | solution.py:16
  182.2 4.5 %fusion.41 = bf16[160,2048]{1,0:T(8,128)(2,1)S(1)} fusion(s32[2048]{0:T(1024)S(1)} %bitcast.211, bf16[6,160,2560]{2,1,0:T(8,128)(2,1)S(1)} %pad_maximum_fusion), kind=kOutput, calls=%fused_computation.58 | convolution fusion | flops 1683292160 | bytes 1482752 | tf_op jit(solution)/shard_map/dot_general | solution.py:34
  186.7 4.5 %fusion.40 = bf16[160,2048]{1,0:T(8,128)(2,1)S(1)} fusion(s32[2048]{0:T(1024)S(1)} %bitcast.210, bf16[6,160,2560]{2,1,0:T(8,128)(2,1)S(1)} %pad_maximum_fusion), kind=kOutput, calls=%fused_computation.57 | convolution fusion | flops 1683292160 | bytes 1482752 | tf_op jit(solution)/shard_map/dot_general | solution.py:34
  191.2 4.5 %fusion.39 = bf16[160,2048]{1,0:T(8,128)(2,1)S(1)} fusion(s32[2048]{0:T(1024)S(1)} %bitcast.209, bf16[6,160,2560]{2,1,0:T(8,128)(2,1)S(1)} %pad_maximum_fusion), kind=kOutput, calls=%fused_computation.56 | convolution fusion | flops 1683292160 | bytes 1482752 | tf_op jit(solution)/shard_map/dot_general | solution.py:34
  195.6 4.6 %fusion.38 = bf16[160,2048]{1,0:T(8,128)(2,1)S(1)} fusion(s32[2048]{0:T(1024)S(1)} %bitcast.208, bf16[6,160,2560]{2,1,0:T(8,128)(2,1)S(1)} %pad_maximum_fusion), kind=kOutput, calls=%fused_computation.55 | convolution fusion | flops 1683292160 | bytes 1482752 | tf_op jit(solution)/shard_map/dot_general | solution.py:34
  200.3 4.5 %fusion.37 = bf16[160,2048]{1,0:T(8,128)(2,1)S(1)} fusion(s32[2048]{0:T(1024)S(1)} %bitcast.207, bf16[6,160,2560]{2,1,0:T(8,128)(2,1)S(1)} %pad_maximum_fusion), kind=kOutput, calls=%fused_computation.54 | convolution fusion | flops 1683292160 | bytes 1482752 | tf_op jit(solution)/shard_map/dot_general | solution.py:34
  204.7 4.5 %fusion.36 = bf16[160,2048]{1,0:T(8,128)(2,1)S(1)} fusion(s32[2048]{0:T(1024)S(1)} %bitcast.206, bf16[6,160,2560]{2,1,0:T(8,128)(2,1)S(1)} %pad_maximum_fusion), kind=kOutput, calls=%fused_computation.53 | convolution fusion | flops 1683292160 | bytes 1482752 | tf_op jit(solution)/shard_map/dot_general | solution.py:34
  209.5 3.5 %fusion.42 = f32[5,2048,125,1]{1,2,3,0:T(8,128)} fusion(bf16[2,5,6,16,2048]{4,3,2,1,0:T(8,128)(2,1)S(1)} %constant_dynamic-update-slice_fusion, bf16[6,125,16]{1,2,0:T(8,128)(2,1)S(1)} %copy-done.7), kind=kOutput, calls=%fused_computation.61 | convolution fusion | flops 245760000 | bytes 7110656 | tf_op jit(solution)/shard_map/yzu,hyui->hzi/dot_general | solution.py:94
  215.9 2.3 reshape.170
  218.2 4.7 %convolution_convert_fusion.1 = bf16[625,512]{1,0:T(8,128)(2,1)} fusion(bf16[625,2048]{1,0:T(8,128)(2,1)} %reshape.170, bf16[2048,512]{1,0:T(8,128)(2,1)} %copy-done.16), kind=kOutput, calls=%fused_computation.70 | convolution fusion | flops 1311040000 | bytes 5297152 | tf_op jit(solution)/shard_map/dot_general | solution.py:123
  222.9 1.4 copy.61
  225.3 9.8 %all-to-all-start = ((bf16[625,128,4]{0,2,1:T(4,128)(2,1)}), bf16[625,128,4]{0,2,1:T(4,128)(2,1)S(1)}, u32[]{:S(2)}, u32[]{:S(2)}) async-start(bf16[625,128,4]{0,2,1:T(4,128)(2,1)} %all_to_all.12), calls=%async_computation | async-start | bytes 1310720 | tf_op jit(solution)/shard_map/all_to_all | solution.py:130
  235.0 10.1 %fusion.27 = f32[2048]{0:T(1024)S(1)} fusion(f32[5,2048,125,1]{1,2,3,0:T(8,128)} %fusion.42, f32[5,2048,125,1]{1,2,0,3:T(8,128)} %fusion.65, bf16[5,125,2048]{2,1,0:T(8,128)(2,1)S(1)} %fusion.28, bf16[1,5,216,2048]{3,2,1,0:T(8,128)(2,1)} %get-tuple-element.8, bf16[1,5,216,2048]{3,2,1,0:T(8,128)(2,1)} %get-tuple-element.7, ...), kind=kOutput, calls=%fused_computation.37 | convolution fusion | flops 1678548992 | bytes 26241232 | tf_op jit(solution)/shard_map/lgy,luyc->ugc/dot_general | solution.py:88
  245.8 2.4 copy.64
  248.2 67.2 %psum.7 = f32[]{:T(128)} all-reduce(f32[]{:T(128)} %abs_reduce_fusion), channel_id=1, replica_groups=mesh['dom'=32,'sub'=4] {'dom','sub'}, use_global_device_ids=true, to_apply=%region_2.3 | all-reduce | flops 1 | bytes 8 | tf_op jit(solution)/shard_map/psum | solution.py:100
  317.4 1.4 copy.63
  (69 shorter events, 20.7 us)
Async XLA Ops:
  0.6 234.4 %copy-start = (bf16[3,125,216]{1,2,0:T(8,128)(2,1)S(1)}, bf16[3,125,216]{1,2,0:T(8,128)(2,1)}, u32[]{:S(2)}) copy-start(bf16[3,125,216]{1,2,0:T(8,128)(2,1)} %param.20) | copy-start | bytes 486004
  0.6 2.9 copy-start.10
  4.8 1.9 copy-start.2
  4.9 12.8 %copy-start.14 = (s32[256,1]{0,1:T(1,128)S(1)}, s32[256,1]{0,1:T(1,128)}, u32[]{:S(2)}) copy-start(s32[256,1]{0,1:T(1,128)} %param.18) | copy-start | bytes 3076
  4.9 13.1 %copy-start.15 = (s32[256]{0:T(256)S(1)}, s32[256]{0:T(256)}, u32[]{:S(2)}) copy-start(s32[256]{0:T(256)} %param.17) | copy-start | bytes 3076
  6.7 1.9 copy-start.3
  6.7 13.4 %copy-start.4 = (bf16[5,64,2048]{2,1,0:T(8,128)(2,1)S(1)}, bf16[5,64,2048]{2,1,0:T(8,128)(2,1)}, u32[]{:S(2)}) copy-start(bf16[5,64,2048]{2,1,0:T(8,128)(2,1)} %param.13) | copy-start | bytes 3932164
  9.7 168.9 %collective-permute-start = (bf16[6,160,256]{2,1,0:T(8,128)(2,1)}, bf16[6,160,256]{2,1,0:T(8,128)(2,1)S(1)}, u32[]{:S(2)}, u32[]{:S(2)}) collective-permute-start(bf16[6,160,256]{2,1,0:T(8,128)(2,1)} %get-tuple-element.12), channel_id=1, source_target_pairs={{0,1},{1,2},{2,3},{3,4},{4,5},{5,6},{6,7},{7,8},{8,9},{9,10},{10,1... | collective-permute-start | bytes 1474568 | tf_op jit(solution)/shard_map/ppermute | solution.py:12
  13.9 164.8 %collective-permute-start.1 = (bf16[6,160,256]{2,1,0:T(8,128)(2,1)}, bf16[6,160,256]{2,1,0:T(8,128)(2,1)}, u32[]{:S(2)}, u32[]{:S(2)}) collective-permute-start(bf16[6,160,256]{2,1,0:T(8,128)(2,1)} %get-tuple-element.13), channel_id=1, source_target_pairs={{1,0},{2,1},{3,2},{4,3},{5,4},{6,5},{7,6},{8,7},{9,8},{10,9},{11,1... | collective-permute-start | bytes 1474568 | tf_op jit(solution)/shard_map/ppermute | solution.py:15
  18.9 1.3 copy-start.16
  20.2 11.7 %copy-start.9 = (s32[2048]{0:T(1024)S(1)}, s32[2048]{0:T(1024)}, u32[]{:S(2)}) copy-start(s32[2048]{0:T(1024)} %param.15) | copy-start | bytes 24580
  21.0 17.0 %copy-start.8 = (bf16[216,64]{0,1:T(8,128)(2,1)S(1)}, bf16[216,64]{0,1:T(8,128)(2,1)}, u32[]{:S(2)}) copy-start(bf16[216,64]{0,1:T(8,128)(2,1)} %param.19) | copy-start | bytes 82948
  22.1 155.1 %all-to-all-start.1 = ((bf16[320,128,4]{0,2,1:T(4,128)(2,1)}), bf16[320,128,4]{0,2,1:T(4,128)(2,1)S(1)}, u32[]{:S(2)}, u32[]{:S(2)}) async-start(bf16[320,128,4]{0,2,1:T(4,128)(2,1)} %all_to_all.14), calls=%async_computation.1 | async-start | bytes 786432 | tf_op jit(solution)/shard_map/all_to_all | solution.py:131
  38.0 1.4 copy-start.13
  39.4 68.7 %copy-start.1 = (f32[5,216,2048]{2,1,0:T(8,128)}, f32[5,216,2048]{2,1,0:T(8,128)S(1)}, u32[]{:S(2)}) copy-start(f32[5,216,2048]{2,1,0:T(8,128)S(1)} %convolution_bitcast_fusion) | copy-start | bytes 26542084
  142.0 32.0 %copy-start.7 = (bf16[6,125,16]{1,2,0:T(8,128)(2,1)S(1)}, bf16[6,125,16]{1,2,0:T(8,128)(2,1)}, u32[]{:S(2)}) copy-start(bf16[6,125,16]{1,2,0:T(8,128)(2,1)} %param.23) | copy-start | bytes 72004
  209.5 3.5 %copy-start.11 = (bf16[6,125,16]{1,2,0:T(8,128)(2,1)S(1)}, bf16[6,125,16]{1,2,0:T(8,128)(2,1)}, u32[]{:S(2)}) copy-start(bf16[6,125,16]{1,2,0:T(8,128)(2,1)} %param.25) | copy-start | bytes 72004
  213.0 1.3 copy-start.5
  213.0 1.6 copy-start.6
  213.0 1.6 copy-start.12
  225.3 91.3 %all-to-all-start = ((bf16[625,128,4]{0,2,1:T(4,128)(2,1)}), bf16[625,128,4]{0,2,1:T(4,128)(2,1)S(1)}, u32[]{:S(2)}, u32[]{:S(2)}) async-start(bf16[625,128,4]{0,2,1:T(4,128)(2,1)} %all_to_all.12), calls=%async_computation | async-start | bytes 1310720 | tf_op jit(solution)/shard_map/all_to_all | solution.py:130
where the time goes:
time: 324 us; the launch traced here: 319 us
  matrix products  154 us (48%)
  blocking collectives  67.2 us (21%)
  other arithmetic  43.1 us (13%)
  starting transfers between devices  27.5 us (8%)
  local copies, waits for them, and re-layouts  26.2 us (8%)
    dot_general x3, matrix products, body(): jnp.einsum('uv,vqe->uqe', flux_jac[direction], values, precision=lax.Prec...  98.5 us
    psum x1, blocking collectives, body(): total = lax.psum(jnp.sum(element_error), ('dom', 'sub'))  67.2 us
    another operation x1, other arithmetic, body(): flux_every_face = jnp.stack(fluxes).astype(jnp.bfloat16)  30.9 us
    dot_general x6, matrix products, lookup(): jnp.dot(windows[face ^ 1], select, preferred_element_type=jnp.float32)  27 us
    unnamed x46, local copies, waits for them, and re-layouts  14.3 us
    dot_general x1, matrix products, body(): jnp.einsum('lgy,luyc->ugc', gradient_operator, flux_every_face, preferred...  10.1 us
    all_to_all x1, starting transfers between devices, body(): lax.all_to_all(send_primal, ('dom', 'sub'), split_axis=1, concat_axis=1,...  9.79 us
    all_to_all x1, starting transfers between devices, body(): lax.all_to_all(send_adjoint, ('dom', 'sub'), split_axis=1, concat_axis=1,...  9.75 us
  transfers between devices with their start and end apart: 4, of which 0 were waited for; matrix products, arithmetic and copies ran while one was open for 51% of the time, Pallas kernels for 0%

commit v1 on v0

v1 whole, which is shorter than its diff:
```python
import jax
import jax.numpy as jnp
from jax import lax
from jax.experimental import pallas as pl
from jax.experimental.pallas import tpu as pltpu
from jax.sharding import PartitionSpec as P

AXES = ("dom", "sub")
F32 = jnp.float32
BF16 = jnp.bfloat16
VMEM = pl.BlockSpec(memory_space=pltpu.VMEM)
SMEM = pl.BlockSpec(memory_space=pltpu.SMEM)
ANY = pl.BlockSpec(memory_space=pl.ANY)
CHUNK = 256
LIMIT = 56 * 1024 * 1024


def dot(a, b):
    return jnp.dot(a, b, preferred_element_type=F32)


def dot_nt(a, b):
    return lax.dot_general(a, b, (((1,), (1,)), ((), ())), preferred_element_type=F32)


def dot_tn(a, b):
    return lax.dot_general(a, b, (((0,), (0,)), ((), ())), preferred_element_type=F32)


def one_hot(row, depth):
    rows = lax.broadcasted_iota(jnp.int32, (depth, row.shape[1]), 0).astype(jnp.int16)
    return jnp.where(rows == row.astype(jnp.int16), jnp.ones((), BF16), jnp.zeros((), BF16))


def span(c, width=CHUNK):
    return pl.ds(pl.multiple_of(c * width, width), width)


def mode_degree(per_side, shape):
    modes = lax.broadcasted_iota(jnp.int32, shape, 0)
    deg_one = modes // (per_side * per_side)
    deg_two = modes // per_side % per_side
    deg_three = modes % per_side
    return jnp.maximum(jnp.maximum(deg_one, deg_two), deg_three)


def main_kernel(
    groups,
    members,
    primal_in,
    adjoint_in,
    order,
    neighbours_in,
    elem_row,
    dest_row,
    self_t,
    faces_t,
    eval_t,
    slope_t,
    lift_t,
    trace_op,
    jacobian,
    received,
    error,
    total,
    primal,
    adjoint,
    neighbours,
    tall,
    wide,
    trace_mix,
    patch,
    evaluate,
    lifted,
    solo,
    paired,
    weights,
    traces,
    halo,
    outside,
    enriched,
    moved,
    send,
    values,
    moments,
    solo_moments,
    pair_moments,
    part,
    sums,
    loaded,
    halo_sent,
    halo_got,
    ship_sent,
    ship_got,
    sum_sent,
    sum_got,
    own_done,
):
    variables, modes, count = primal.shape
    high_count = self_t.shape[1]
    high_modes = enriched.shape[1]
    quad = eval_t.shape[1]
    padded = evaluate.shape[0]
    stacked = trace_op.shape[0]
    points = stacked // 6
    half = variables * points
    chunks = count // CHUNK
    devices = groups * members
    moves = elem_row.shape[1]
    slots = 4 * devices
    faces = 3 * padded
    share = devices // chunks
    step = 32
    pairs = ((1, 2), (2, 3), (1, 3))

    dom = lax.axis_index("dom")
    sub = lax.axis_index("sub")
    me = dom * members + sub

    def peer(offset):
        other = lax.rem(me + offset, devices)
        return other, (lax.div(other, members), lax.rem(other, members))

    def for_peers(c, act):
        for i in range(1, share):
            act(c * share + i)

        @pl.when(c < chunks - 1)
        def _():
            act(c * share + share)

    barrier = pltpu.get_barrier_semaphore()
    loads = [
        pltpu.make_async_copy(source, target, loaded.at[i])
        for i, (source, target) in enumerate(
            ((adjoint_in, adjoint), (primal_in, primal), (neighbours_in, neighbours))
        )
    ]
    for load in loads:
        load.start()

    @pl.loop(1, devices)
    def _(i):
        pl.semaphore_signal(barrier, inc=1, device_id=peer(i)[1])

    tall[...] = jnp.zeros_like(tall)
    tall[0:modes, 0:high_count] = self_t[...].astype(F32)
    tall[modes : modes + stacked, 0:high_count] = faces_t[...].astype(F32)
    patch[...] = tall[...].T.astype(BF16)
    trace_mix[...] = jnp.zeros_like(trace_mix)
    for v in range(4):
        trace_mix[v * stacked : (v + 1) * stacked, v * modes : (v + 1) * modes] = trace_op[...]

    low = mode_degree(4, (modes, CHUNK))
    high = mode_degree(5, (high_modes, CHUNK))

    def keep_low(at):
        return (low <= order[:, at]).astype(F32).astype(BF16)

    def trace(c, kind):
        at = pl.ds(c * CHUNK, CHUNK) if isinstance(c, int) else span(c)
        keep = keep_low(at)
        fields = [(primal, adjoint)[kind][v, :, at] * keep for v in range(variables)]
        for first in range(0, variables, 4):
            group = fields[first : first + 4]
            mixed = dot(
                trace_mix[: len(group) * stacked, : len(group) * modes],
                jnp.concatenate(group, axis=0) if len(group) > 1 else group[0],
            ).astype(BF16)
            for g in range(len(group)):
                row = (kind * variables + first + g) * points
                for f in range(6):
                    start = g * stacked + f * points
                    traces[f, c, row : row + points, :] = mixed[start : start + points]

    def halo_copy(side):
        return pltpu.make_async_remote_copy(
            src_ref=traces.at[5, chunks - 1] if side == 0 else traces.at[4, 0],
            dst_ref=halo.at[side],
            send_sem=halo_sent.at[side],
            recv_sem=halo_got.at[side],
            device_id=peer(1 if side == 0 else devices - 1)[1],
        )

    def gather(c, kind):
        at = span(c)
        for f in range(6):
            index = neighbours[f : f + 1, at] - CHUNK
            block = (index >> 8).astype(jnp.int16)
            table = traces[f ^ 1, :, kind * half : (kind + 1) * half, :]
            table = table.reshape(chunks * half, CHUNK)
            found = dot(table, one_hot(index & (CHUNK - 1), CHUNK)).astype(BF16)
            picked = jnp.zeros((half, CHUNK), BF16)
            for a in range(chunks):
                here = block == jnp.int16(a)
                picked = jnp.where(here, found[a * half : (a + 1) * half], picked)
            for v in range(variables):
                outside[kind * variables + v, f * points : (f + 1) * points, at] = picked[
                    v * points : (v + 1) * points
                ]

    def gather_halo(kind):
        for side, f, start, wanted in ((0, 4, 0, -1), (1, 5, count - CHUNK, chunks)):
            index = neighbours[f : f + 1, start : start + CHUNK] - CHUNK
            found = dot(halo[side, kind * half : (kind + 1) * half, :], one_hot(index & (CHUNK - 1), CHUNK))
            found = jnp.where((index >> 8) == wanted, found, 0.0).astype(BF16)
            for v in range(variables):
                place = (
                    kind * variables + v,
                    pl.ds(f * points, points),
                    pl.ds(start, CHUNK),
                )
                outside[place] = outside[place] + found[v * points : (v + 1) * points]

    named = one_hot(dest_row[...], devices)
    earlier = lax.broadcasted_iota(jnp.int32, (moves, moves), 0) < lax.broadcasted_iota(
        jnp.int32, (moves, moves), 1
    )
    before = dot(named, earlier.astype(F32).astype(BF16))
    rank = jnp.sum(before * named.astype(F32), axis=0, keepdims=True).astype(jnp.int32)
    slot = dest_row[...] * 4 + rank
    block_of = (elem_row[...] >> 8).astype(jnp.int16)
    low_of = elem_row[...] & (CHUNK - 1)

    def move(rows_of):
        pick = one_hot(low_of, CHUNK)
        held = None
        for a in range(chunks):
            found = dot(rows_of(pl.ds(a * CHUNK, CHUNK)), pick).astype(BF16)
            held = jnp.zeros_like(found) if held is None else held
            held = jnp.where(block_of == jnp.int16(a), found, held)
        return held

    def ship(i):
        other, target = peer(i)
        return pltpu.make_async_remote_copy(
            src_ref=send.at[other],
            dst_ref=received.at[me],
            send_sem=ship_sent,
            recv_sem=ship_got,
            device_id=target,
        )

    loads[0].wait()

    @pl.loop(0, chunks // 2)
    def _(c):
        for b in range(2):
            trace(2 * c + b, 1)

    loads[1].wait()
    loads[2].wait()
    trace(0, 0)
    trace(chunks - 1, 0)

    primal_rows = variables * high_modes
    moved[primal_rows : primal_rows + variables * modes, :] = move(
        lambda at: primal[:, :, at].reshape(variables * modes, CHUNK)
    )
    moved[primal_rows + variables * modes :, :] = jnp.zeros(
        (moved.shape[0] - primal_rows - variables * modes, moves), BF16
    )

    pl.semaphore_wait(barrier, devices - 1)
    for side in range(2):
        halo_copy(side).start()

    @pl.loop(0, chunks)
    def _(c):
        gather(c, 1)

    for side in range(2):
        halo_copy(side).wait_recv()
    gather_halo(1)

    def enrich(c):
        at = span(c)
        keep = keep_low(at)
        keep_high = (high <= order[:, at] + 1).astype(F32)
        for v in range(variables):
            own = adjoint[v, :, at] * keep
            both = jnp.concatenate([own, outside[variables + v, :, at]], axis=0)
            enriched[v, :, at] = (keep_high * dot(patch[:, : modes + stacked], both)).astype(BF16)

    @pl.loop(0, chunks // 2)
    def _(c):
        for b in range(2):
            enrich(2 * c + b)

    moved[:primal_rows, :] = move(
        lambda at: enriched[:, :, at].reshape(variables * high_modes, CHUNK)
    )
    place = one_hot(slot, slots)
    for j in range(0, 8, 2):
        pair = dot_nt(place, moved[j * 128 : (j + 2) * 128, :])
        for h in range(2):
            block = pair[:, h * 128 : (h + 1) * 128].reshape(devices, 4, 128)
            send[:, j + h] = block.astype(BF16)
    own = pltpu.make_async_copy(send.at[me], received.at[me], own_done)
    own.start()

    @pl.loop(0, chunks)
    def _(c):
        for_peers(c, lambda i: ship(i).start())

    @pl.loop(0, chunks // 2 - 1)
    def _(c):
        for b in range(2):
            trace(2 * c + 1 + b, 0)

    @pl.loop(0, chunks)
    def _(c):
        gather(c, 0)

    gather_halo(0)

    wide[...] = jnp.zeros_like(wide)
    wide[0:modes, 0:quad] = eval_t[...].astype(F32)
    evaluate[...] = wide[...].T[:padded, :modes].astype(BF16)
    lifted[...] = jnp.zeros_like(lifted)
    for d in range(3):
        lifted[d * padded : d * padded + quad, 0:high_count] = slope_t[d]
    lifted[faces : faces + stacked, 0:high_count] = lift_t[...]
    for d in range(3):
        solo[d, :padded, :] = lifted[d * padded : (d + 1) * padded, :]
        solo[d, padded:, :] = lifted[faces:, :]
    for p, (i, j) in enumerate(pairs):
        paired[p, :, :high_modes] = lifted[(j - 1) * padded : j * padded, :]
        paired[p, :, high_modes:] = lifted[(i - 1) * padded : i * padded, :]

    direct = dot_tn(trace_op[...], lifted[faces : faces + stacked, :])
    slopes = [dot(eval_t[...], lifted[d * padded : d * padded + quad, :]) for d in range(3)]
    for v in range(variables):
        for u in range(variables):
            block = jacobian[u, 0, v] * slopes[0]
            for d in range(1, 3):
                block = block + jacobian[u, d, v] * slopes[d]
            if u == v:
                block = block + direct
            weights[v * modes : (v + 1) * modes, u * high_modes : (u + 1) * high_modes] = (
                block.astype(BF16)
            )

    def errors(c, values, moments, solo_moments, pair_moments):
        at = span(c)
        keep = keep_low(at)
        every = enriched[:, :, at].reshape(variables * high_modes, CHUNK)
        linear = dot(weights[...], every)
        summed = jnp.zeros((step, CHUNK), F32)
        for v in range(variables):
            own = primal[v, :, at] * keep
            values[v] = dot(evaluate[...], own)
            for r in range(0, modes, step):
                summed = summed + own[r : r + step].astype(F32) * linear[
                    v * modes + r : v * modes + r + step
                ]
        for e, u in enumerate((0, 4)):
            moments[e] = dot(lifted[...], enriched[u, :, at])
        for u in range(1, 4):
            solo_moments[u - 1] = dot(solo[u - 1], enriched[u, :, at])
        for p, (i, j) in enumerate(pairs):
            both = jnp.concatenate([enriched[i, :, at], enriched[j, :, at]], axis=0)
            pair_moments[p] = dot(paired[p], both)
        for r in range(0, stacked, step):
            for u in range(variables):
                if u in (0, 4):
                    lift = moments[u // 4, faces + r : faces + r + step]
                else:
                    lift = solo_moments[u - 1, padded + r : padded + r + step]
                summed = summed - outside[u, r : r + step, at].astype(F32) * lift
        for r in range(0, padded, step):
            here = [values[v, r : r + step] for v in range(variables)]
            for d in range(3):
                row = d * padded + r
                inner = here[0] * moments[0, row : row + step]
                inner = inner + here[4] * moments[1, row : row + step]
                inner = inner + here[d + 1] * solo_moments[d, r : r + step]
                for p, (i, j) in enumerate(pairs):
                    if i == d + 1:
                        inner = inner + here[j] * pair_moments[p, r : r + step]
                summed = summed + (0.25 * here[d + 1]) * inner
        error[:, at] = jnp.abs(jnp.sum(summed, axis=0, keepdims=True))

    @pl.loop(0, chunks // 2)
    def _(c):
        for b in range(2):
            errors(2 * c + b, values.at[b], moments.at[b], solo_moments.at[b], pair_moments.at[b])

    mine = error[:, 0:128]
    for r in range(128, count, 128):
        mine = mine + error[:, r : r + 128]
    part[...] = mine
    sums[me] = mine

    def tell(i):
        return pltpu.make_async_remote_copy(
            src_ref=part,
            dst_ref=sums.at[me],
            send_sem=sum_sent,
            recv_sem=sum_got,
            device_id=peer(i)[1],
        )

    @pl.loop(1, devices)
    def _(i):
        tell(i).start()

    def every_other(ref, sent, got):
        others = ref.at[pl.ds(0, devices - 1)]
        return pltpu.make_async_remote_copy(
            src_ref=others, dst_ref=others, send_sem=sent, recv_sem=got, device_id=peer(1)[1]
        )

    waits = [
        every_other(received, ship_sent, ship_got),
        every_other(sums, sum_sent, sum_got),
    ]
    own.wait()
    for wait in waits:
        wait.wait_recv()
    whole = jnp.sum(jnp.sum(sums[...], axis=0), axis=1, keepdims=True)
    total[...] = jnp.broadcast_to(whole, total.shape)
    for wait in waits:
        wait.wait_send()
    for side in range(2):
        halo_copy(side).wait_send()


def unpack_kernel(
    elements, received, error, total, indicator, shipped_adjoint, shipped_primal
):
    variables, high_modes, slots = shipped_adjoint.shape
    modes = shipped_primal.shape[1]
    share = error[...] * elements / total[:, 0:1]
    for r in range(indicator.shape[0]):
        indicator[r : r + 1, :] = share[:, r * 128 : (r + 1) * 128]

    def columns(j):
        return received[:, j].astype(F32).reshape(slots, 128).T.astype(BF16)

    for j in range(variables):
        shipped_adjoint[j] = columns(j)[:high_modes]
    for j in range(3):
        block = columns(variables + j)
        shipped_primal[2 * j] = block[:modes]
        if 2 * j + 1 < variables:
            shipped_primal[2 * j + 1] = block[modes:]


def call(kernel, out_shape, in_specs, out_specs, scratch=(), **params):
    return pl.pallas_call(
        kernel,
        out_shape=out_shape,
        in_specs=in_specs,
        out_specs=out_specs,
        scratch_shapes=scratch,
        compiler_params=pltpu.CompilerParams(vmem_limit_bytes=LIMIT, **params),
    )


def body(
    primal,
    adjoint,
    order,
    faces_nbr,
    move_elem,
    move_dest,
    eval_op,
    gradient_operator,
    flux_jac,
    trace_op,
    lifting_operator,
    patch_from_self,
    patch_from_faces,
):
    variables, modes, count = primal.shape
    points = trace_op.shape[1]
    stacked = 6 * points
    half = variables * points
    chunks = count // CHUNK
    groups = lax.axis_size("dom")
    members = lax.axis_size("sub")
    devices = groups * members
    moves = move_elem.shape[0]
    slots = 4 * devices
    high = patch_from_self.shape[0]
    high_pad = 128
    quad_pad = 224
    shape = jax.ShapeDtypeStruct
    dma = pltpu.SemaphoreType.DMA

    received, error, total = call(
        lambda *refs: main_kernel(groups, members, *refs),
        (
            shape((devices, 8, 4, 128), BF16),
            shape((1, count), F32),
            shape((1, 128), F32),
        ),
        [ANY, ANY, VMEM, ANY] + [VMEM] * 8 + [SMEM],
        [ANY, VMEM, VMEM],
        [
            pltpu.VMEM(primal.shape, BF16),
            pltpu.VMEM(adjoint.shape, BF16),
            pltpu.VMEM(faces_nbr.shape, jnp.int32),
            pltpu.VMEM((256, high_pad), F32),
            pltpu.VMEM((128, 256), F32),
            pltpu.VMEM((4 * stacked, 4 * modes), BF16),
            pltpu.VMEM((high_pad, 256), BF16),
            pltpu.VMEM((quad_pad, modes), BF16),
            pltpu.VMEM((3 * quad_pad + stacked, high_pad), BF16),
            pltpu.VMEM((3, quad_pad + stacked, high_pad), BF16),
            pltpu.VMEM((3, quad_pad, 2 * high_pad), BF16),
            pltpu.VMEM((variables * modes, variables * high_pad), BF16),
            pltpu.VMEM((6, chunks, 2 * half, CHUNK), BF16),
            pltpu.VMEM((2, 2 * half, CHUNK), BF16),
            pltpu.VMEM((2 * variables, stacked, count), BF16),
            pltpu.VMEM((variables, high_pad, count), BF16),
            pltpu.VMEM((1024, moves), BF16),
            pltpu.VMEM((devices, 8, 4, 128), BF16),
            pltpu.VMEM((2, variables, quad_pad, CHUNK), F32),
            pltpu.VMEM((2, 2, 3 * quad_pad + stacked, CHUNK), F32),
            pltpu.VMEM((2, 3, quad_pad + stacked, CHUNK), F32),
            pltpu.VMEM((2, 3, quad_pad, CHUNK), F32),
            pltpu.VMEM((1, 128), F32),
            pltpu.VMEM((devices, 1, 128), F32),
            dma((3,)),
            dma((2,)),
            dma((2,)),
            dma,
            dma,
            dma,
            dma,
            dma,
        ],
        collective_id=0,
        has_side_effects=True,
    )(
        primal,
        adjoint,
        order.reshape(1, count),
        faces_nbr,
        move_elem.reshape(1, moves),
        move_dest.reshape(1, moves),
        patch_from_self.T,
        patch_from_faces.transpose(0, 2, 1).reshape(stacked, high),
        eval_op.T,
        gradient_operator.transpose(0, 2, 1),
        lifting_operator.transpose(0, 2, 1).reshape(stacked, high),
        trace_op.reshape(stacked, modes),
        flux_jac.transpose(1, 0, 2),
    )

    indicator, shipped_adjoint, shipped_primal = call(
        lambda *refs: unpack_kernel(count * devices, *refs),
        (
            shape((count // 128, 128), F32),
            shape((variables, high, slots), BF16),
            shape((variables, modes, slots), BF16),
        ),
        [VMEM] * 3,
        [VMEM] * 3,
    )(received, error, total)
    return (indicator.reshape(count), shipped_adjoint, shipped_primal)


def solution(mesh):
    return jax.shard_map(
        body,
        mesh=mesh,
        in_specs=(
            P(None, None, AXES),
            P(None, None, AXES),
            P(AXES),
            P(None, AXES),
            P(AXES),
            P(AXES, None),
            P(),
            P(),
            P(),
            P(),
            P(),
            P(),
            P(),
        ),
        out_specs=(P(AXES), P(None, None, AXES), P(None, None, AXES)),
        check_vma=False,
    )
```

time: 324 us -> 45.3 us (0.14); the launches traced: 319 us -> 45.1 us
  matrix products: 154 us -> 0 us
  blocking collectives: 67.2 us -> 0 us
  Pallas kernels: 0 us -> 44.5 us
  other arithmetic: 43.1 us -> 0 us
  starting transfers between devices: 27.5 us -> 0 us
  local copies, waits for them, and re-layouts: 26.2 us -> 0 us
    dot_general x20 -> x0, matrix products: 154 us -> none  [the longest x3 98.5 us: body(): jnp.einsum('uv,vqe->uqe', flux_jac[direction], values, precision=lax.Prec...]
    psum x1 -> x0, blocking collectives: 67.2 us -> none  [body(): total = lax.psum(jnp.sum(element_error), ('dom', 'sub'))]
    pallas_call x0 -> x2, Pallas kernels: none -> 44.5 us  [the longest x1 42 us: body(): call(lambda *refs: main_kernel(groups, members, *refs), (shape((devices,...]
    another operation x2 -> x0, other arithmetic: 32.9 us -> none  [the longest x1 30.9 us: body(): flux_every_face = jnp.stack(fluxes).astype(jnp.bfloat16)]
    all_to_all x2 -> x0, starting transfers between devices: 19.5 us -> none  [the longest x1 9.79 us: body(): lax.all_to_all(send_primal, ('dom', 'sub'), split_axis=1, concat_axis=1,...]
    unnamed x46 -> x0, local copies, waits for them, and re-layouts: 14.3 us -> none
    ppermute x2 -> x0, starting transfers between devices: 7.94 us -> none  [the longest x1 4.11 us: with_halo(): lax.ppermute(lax.slice_in_dim(block, block.shape[dim] - width, None, axis...]
    reshape x3 -> x0, local copies, waits for them, and re-layouts: 4.55 us -> none  [the longest x1 2.27 us: body(): adjoint_rows = enriched_adjoint.reshape(-1, count)]
  transfers between devices with their start and end apart: 4 -> 0, of which waited for: 0 -> 0; matrix products, arithmetic and copies ran while one was open for 51% -> 0% of each run, Pallas kernels for 0% -> 0%
where the time goes in v1:
time: 45.3 us; the launch traced here: 45.1 us
  Pallas kernels  44.5 us (98%)
  between operations  0.64 us (1%)
    pallas_call x1, Pallas kernels, body(): call(lambda *refs: main_kernel(groups, members, *refs), (shape((devices,...  42 us
    pallas_call x1, Pallas kernels, body(): call(lambda *refs: unpack_kernel(count * devices, *refs), (shape((count /...  2.48 us

profile of v1, /device:TPU:1, one launch (start us, length us, event | category | flops | bytes accessed | tf_op | source)
XLA Modules:
  0.0 45.1 jit_solution(333887612623366210)
XLA Ops:
  0.6 42.0 %shard_map.148 = (bf16[128,8,4,128]{3,2,1,0:T(4,128)(2,1)}, f32[1,2048]{1,0:T(1,128)}, f32[1,128]{1,0:T(1,128)}) custom-call(bf16[5,64,2048]{2,1,0:T(8,128)(2,1)} %refs_0_.1, bf16[5,64,2048]{2,1,0:T(8,128)(2,1)} %refs_1_.1, s32[1,2048]{1,0:T(1,128)} %bitcast.22, s32[6,2048]{1,0:T(8,128)} %refs_3_.1, s32[1,256]{1,0:T(1,128)} %bitcast.23, s32[1,256]{1,0:T(1,128)} %bitcast.24, ...), custom_call_target="tpu_custom_call" | custom-call | tf_op jit(solution)/shard_map/pallas_call | solution.py:492
  42.6 2.5 %shard_map.149 = (f32[16,128]{1,0:T(8,128)}, bf16[5,125,512]{2,1,0:T(8,128)(2,1)}, bf16[5,64,512]{2,1,0:T(8,128)(2,1)}) custom-call(bf16[128,8,4,128]{3,2,1,0:T(4,128)(2,1)} %get-tuple-element.9.refs_0_, f32[1,2048]{1,0:T(1,128)} %get-tuple-element.10.refs_1_, f32[1,128]{1,0:T(1,128)} %get-tuple-element.11.refs_2_), custom_call_target="tpu_custom_call" | custom-call | tf_op jit(solution)/shard_map/pallas_call | solution.py:553

commit v2 on v1

--- a/solution.py
+++ b/solution.py
@@ -265,9 +265,10 @@
     for side in range(2):
         halo_copy(side).start()
 
-    @pl.loop(0, chunks)
-    def _(c):
-        gather(c, 1)
+    @pl.loop(0, chunks // 2)
+    def _(c):
+        for b in range(2):
+            gather(2 * c + b, 1)
 
     for side in range(2):
         halo_copy(side).wait_recv()
@@ -308,9 +309,10 @@
         for b in range(2):
             trace(2 * c + 1 + b, 0)
 
-    @pl.loop(0, chunks)
-    def _(c):
-        gather(c, 0)
+    @pl.loop(0, chunks // 2)
+    def _(c):
+        for b in range(2):
+            gather(2 * c + b, 0)
 
     gather_halo(0)
 

time: 45.3 us -> 44 us (0.971)
  Pallas kernels: 44.5 us -> 43.2 us
    pallas_call x1, Pallas kernels: 42 us -> 40.7 us  [body(): call(lambda *refs: main_kernel(groups, members, *refs), (shape((devices,...]
where the time goes in v2:
time: 44 us; the launch traced here: 43.8 us
  Pallas kernels  43.2 us (98%)
  between operations  0.64 us (1%)
    pallas_call x1, Pallas kernels, body(): call(lambda *refs: main_kernel(groups, members, *refs), (shape((devices,...  40.7 us
    pallas_call x1, Pallas kernels, body(): call(lambda *refs: unpack_kernel(count * devices, *refs), (shape((count /...  2.48 us

profile of v2, /device:TPU:1, one launch (start us, length us, event | category | flops | bytes accessed | tf_op | source)
XLA Modules:
  0.0 43.8 jit_solution(15316079405424074743)
XLA Ops:
  0.6 40.7 %shard_map.148 = (bf16[128,8,4,128]{3,2,1,0:T(4,128)(2,1)}, f32[1,2048]{1,0:T(1,128)}, f32[1,128]{1,0:T(1,128)}) custom-call(bf16[5,64,2048]{2,1,0:T(8,128)(2,1)} %refs_0_.1, bf16[5,64,2048]{2,1,0:T(8,128)(2,1)} %refs_1_.1, s32[1,2048]{1,0:T(1,128)} %bitcast.22, s32[6,2048]{1,0:T(8,128)} %refs_3_.1, s32[1,256]{1,0:T(1,128)} %bitcast.23, s32[1,256]{1,0:T(1,128)} %bitcast.24, ...), custom_call_target="tpu_custom_call" | custom-call | tf_op jit(solution)/shard_map/pallas_call | solution.py:494
  41.4 2.5 %shard_map.149 = (f32[16,128]{1,0:T(8,128)}, bf16[5,125,512]{2,1,0:T(8,128)(2,1)}, bf16[5,64,512]{2,1,0:T(8,128)(2,1)}) custom-call(bf16[128,8,4,128]{3,2,1,0:T(4,128)(2,1)} %get-tuple-element.9.refs_0_, f32[1,2048]{1,0:T(1,128)} %get-tuple-element.10.refs_1_, f32[1,128]{1,0:T(1,128)} %get-tuple-element.11.refs_2_), custom_call_target="tpu_custom_call" | custom-call | tf_op jit(solution)/shard_map/pallas_call | solution.py:555
